TPU v7x, 256 devices: a whole 4x4x8 slice. The times are simulated.
256 devices in a mesh: arc: 16 (over x, y_lo, core), par: 16 (over y_hi, z).
Axes of the slice: x: 4, y: 4 (y_hi: 2, y_lo: 2; y = y_hi * 2 + y_lo), z: 8, core: 2. Of those that a mesh axis runs over, the one named last changes fastest.
Arguments:
- partials: bfloat16 [16, 3, 128, 8192], P('arc', None, 'par'), may hold values from -6 to 6
- epoch_index: int32 [16, 128], P('arc'), may hold values from 0 to 511, as said below
- whitening: float32 [16, 3, 128, 128], P('arc'), may hold values from -2 to 2, as said below
Outputs:
- normal_matrix: float32 [8192, 8192], P('arc', 'par')
Inputs may be any that keep to these rules, and one draw needn't show every extreme that they name: `epoch_index`: in each arc the epoch indices rise strictly; the first is 0 and the last is 511. `whitening`: each block is lower triangular with diagonal entries between 1 and 2.
All inputs are finite; a program needn't handle non-finite values.
Results may differ from a plain program's by a relative error of at most 0.0003.
Values may be sent and summed in bfloat16 or wider, within the bound.
A program may use at most 128 MiB of HBM per device.

v0:
```python
import math
import jax
import jax.numpy as jnp
from jax import lax
from jax.sharding import PartitionSpec as P

KERNEL_GAIN = 8.0


def from_root(block, axis, owner):
    block = jnp.where(lax.axis_index(axis) == owner, block, jnp.zeros_like(block))
    return lax.psum(block, axis)


def mixing_matrices(epoch_index, whitening, epochs, row_scale):
    times_arc = epoch_index.astype(jnp.float32) / jnp.float32(4 * epochs - 1)
    later_time = times_arc[:, :, None]
    earlier_time = times_arc[:, None, :]
    green_part = jnp.minimum(later_time, earlier_time) * (
        1.0 - jnp.maximum(later_time, earlier_time)
    )
    kernel = jnp.eye(epochs, dtype=jnp.float32)[None] + KERNEL_GAIN / epochs * green_part
    mixing = jnp.einsum("acij,ajk->acik", whitening, kernel, precision=lax.Precision.HIGHEST)
    return mixing * row_scale


def on_device(partials, epoch_index, whitening):
    arc_local = partials.shape[0]
    epochs = epoch_index.shape[1]
    param_count = partials.shape[3]
    arc_count = lax.axis_size("arc")
    par_count = lax.axis_size("par")
    total_arcs = arc_local * arc_count
    col_block = param_count // par_count
    row_block = param_count // arc_count
    row_scale = 1.0 / math.sqrt(3 * epochs * total_arcs)
    mixing = mixing_matrices(epoch_index, whitening, epochs, row_scale)
    columns = lax.all_to_all(partials, "par", split_axis=3, concat_axis=2, tiled=True)
    arc_position = lax.axis_index("arc")
    holder = arc_position * row_block // col_block
    gathered = jnp.einsum(
        "acij,acjk->acik", mixing, columns.astype(jnp.float32), precision=lax.Precision.HIGHEST
    )
    gathered = lax.all_gather(gathered, "arc", axis=0, tiled=True)
    row_data = from_root(gathered, "par", holder)
    row_flat = row_data.reshape(-1, row_block)
    col_flat = gathered.reshape(-1, col_block)
    return lax.dot_general(
        row_flat,
        col_flat,
        (((0,), (0,)), ((), ())),
        precision=lax.Precision.HIGHEST,
        preferred_element_type=jnp.float32,
    )


def solution(mesh):
    placed = (P("arc", None, "par", None), P("arc", None), P("arc", None, None, None))
    return jax.shard_map(
        on_device, mesh=mesh, in_specs=placed, out_specs=P("arc", "par"), check_vma=False
    )
```

profile of v0, /device:TPU:1, one launch (start us, length us, event | category | flops | bytes accessed | tf_op | source)
XLA Modules:
  0.0 480.0 jit_solution(4543148357410827872)
XLA Ops:
  6.5 0.0 copy-start
  6.5 0.0 copy-start.1
  6.5 9.5 %copy.5 = bf16[1,3,8,8192]{2,1,0,3:T(4,128)(2,1)} copy(bf16[1,3,8,8192]{3,2,1,0:T(8,128)(2,1)} %param.3) | data formatting | bytes 786432 | tf_op args[0]
  16.1 13.6 %reshape.224 = bf16[16,2,6144]{2,1,0:T(2,128)(2,1)} reshape(bf16[8192,1,3,8]{3,2,1,0:T(4,128)(2,1)} %bitcast.30) | data formatting | bytes 786432
  29.7 11.7 %all-to-all-start = ((bf16[16,2,6144]{2,1,0:T(2,128)(2,1)}), bf16[16,2,6144]{2,1,0:T(2,128)(2,1)S(1)}, u32[]{:S(2)}, u32[]{:S(2)}) async-start(bf16[16,2,6144]{2,1,0:T(2,128)(2,1)} %reshape.224), calls=%async_computation | async-start | bytes 786432 | tf_op jit(solution)/shard_map/all_to_all | solution.py:38
  41.4 0.0 all-gather.3.cloned.1.call-start
  41.5 0.0 copy-done.1
  41.5 0.2 fusion.4
  41.7 0.0 copy-done
  41.7 0.3 fusion
  42.0 11.6 %all-to-all-done = bf16[16,2,6144]{2,1,0:T(2,128)(2,1)S(1)} async-done(((bf16[16,2,6144]{2,1,0:T(2,128)(2,1)}), bf16[16,2,6144]{2,1,0:T(2,128)(2,1)S(1)}, u32[]{:S(2)}, u32[]{:S(2)}) %all-to-all-start) | async-done | bytes 393248 | tf_op jit(solution)/shard_map/all_to_all | solution.py:38
  53.7 10.7 %reshape.225 = bf16[8192,1,3,8]{3,2,1,0:T(4,128)(2,1)} reshape(bf16[16,2,6144]{2,1,0:T(2,128)(2,1)S(1)} %all-to-all-done) | data formatting | bytes 786432
  64.3 10.4 %copy.6 = bf16[1,3,8,16,512]{4,2,3,1,0:T(8,128)(2,1)S(1)} copy(bf16[1,3,8,16,512]{2,1,4,3,0:T(4,128)(2,1)} %bitcast.29) | data formatting | bytes 786432 | tf_op jit(solution)/shard_map/all_to_all | solution.py:38
  74.8 1.4 fusion.1
  76.1 0.0 all-gather.3.cloned.1.call-update
  76.2 0.0 all-reduce.2.cloned.1.call-start
  76.2 73.7 %all-gather.3.cloned.1.call-done = f32[48,128,512]{2,1,0:T(8,128)} async-done(((f32[3,128,512]{2,1,0:T(8,128)}), f32[48,128,512]{2,1,0:T(8,128)}) %all-gather.3.cloned.1.call-update) | async-done | bytes 12582928 | tf_op jit(solution)/shard_map/all_gather | solution.py:44
  149.9 7.3 %broadcast_select_fusion = f32[16,3,128,512]{3,2,1,0:T(8,128)} fusion(f32[16,3,128,512]{3,2,1,0:T(8,128)} %bitcast.27, pred[]{:T(512)S(6)} %eq.21), kind=kLoop, calls=%fused_computation | loop fusion | flops 3145728 | bytes 25165824 | tf_op jit(solution)/shard_map/jit(_where)/select_n | solution.py:11
  157.2 0.0 all-reduce.2.cloned.1.call-update
  157.3 291.5 %all-reduce.2.cloned.1.call-done = f32[16,3,128,512]{3,2,1,0:T(8,128)} async-done(((f32[16,3,128,512]{3,2,1,0:T(8,128)}), f32[16,3,128,512]{3,2,1,0:T(8,128)}) %all-reduce.2.cloned.1.call-update) | async-done | bytes 12582928 | tf_op jit(solution)/shard_map/psum | solution.py:12
  448.8 24.4 %convolution_bitcast_fusion = f32[512,512]{1,0:T(8,128)} fusion(f32[16,3,128,512]{3,2,1,0:T(8,128)} %all-reduce.2.cloned.1.call-done, f32[16,3,128,512]{3,2,1,0:T(8,128)} %bitcast.28), kind=kOutput, calls=%fused_computation.1 | convolution fusion | flops 19327352832 | bytes 26214400 | tf_op jit(solution)/shard_map/dot_general | solution.py:48
  (1 shorter events, 0.0 us)
Async XLA Ops:
  6.5 35.2 %copy-start = (f32[1,3,128,128]{3,2,1,0:T(8,128)S(1)}, f32[1,3,128,128]{3,2,1,0:T(8,128)}, u32[]{:S(2)}) copy-start(f32[1,3,128,128]{3,2,1,0:T(8,128)} %param.5) | copy-start | bytes 589828
  6.5 34.9 %copy-start.1 = (s32[1,128]{1,0:T(1,128)S(1)}, s32[1,128]{1,0:T(1,128)}, u32[]{:S(2)}) copy-start(s32[1,128]{1,0:T(1,128)} %param.4) | copy-start | bytes 1540
  29.7 24.0 %all-to-all-start = ((bf16[16,2,6144]{2,1,0:T(2,128)(2,1)}), bf16[16,2,6144]{2,1,0:T(2,128)(2,1)S(1)}, u32[]{:S(2)}, u32[]{:S(2)}) async-start(bf16[16,2,6144]{2,1,0:T(2,128)(2,1)} %reshape.224), calls=%async_computation | async-start | bytes 786432 | tf_op jit(solution)/shard_map/all_to_all | solution.py:38
  41.4 108.5 %all-gather.3.cloned.1.call-start = ((), (), s32[]{:S(2)}) async-start(), calls=%async_computation.2 | async-start | bytes 13369344 | tf_op jit(solution)/shard_map/all_gather | solution.py:44
  76.2 372.6 %all-reduce.2.cloned.1.call-start = ((), (), s32[]{:S(2)}) async-start(), calls=%async_computation.1 | async-start | bytes 25165824 | tf_op jit(solution)/shard_map/psum | solution.py:12
Sparse Core Ops, SparseCore 0:
  76.3 73.5 all-gather.2
  157.4 291.3 all-reduce.1
where the time goes:
time: 482 us; the launch traced here: 480 us
  waiting for transfers between devices  377 us (78%)
  local copies, waits for them, and re-layouts  44.2 us (9%)
  matrix products  26.1 us (5%)
  between operations  13.5 us (3%)
  starting transfers between devices  11.8 us (2%)
  other arithmetic  7.55 us (2%)
    psum x1, waiting for transfers between devices, from_root(): return lax.psum(block, axis)  292 us
    all_gather x1, waiting for transfers between devices, on_device(): gathered = lax.all_gather(gathered, 'arc', axis=0, tiled=True)  73.7 us
    unnamed x7, local copies, waits for them, and re-layouts  33.8 us
    dot_general x1, matrix products, on_device(): lax.dot_general(row_flat, col_flat, (((0,), (0,)), ((), ())), precision=l...  24.4 us
    all_to_all x1, starting transfers between devices, on_device(): lax.all_to_all(partials, 'par', split_axis=3, concat_axis=2, tiled=True)  11.7 us
    all_to_all x1, waiting for transfers between devices, on_device(): lax.all_to_all(partials, 'par', split_axis=3, concat_axis=2, tiled=True)  11.6 us
    all_to_all x1, local copies, waits for them, and re-layouts, on_device(): lax.all_to_all(partials, 'par', split_axis=3, concat_axis=2, tiled=True)  10.4 us
  transfers between devices with their start and end apart: 3, of which 3 were waited for; matrix products, arithmetic and copies ran while one was open for 0% of the time, Pallas kernels for 0%

commit v1 on v0

--- a/solution.py
+++ b/solution.py
@@ -41,7 +41,9 @@
     gathered = jnp.einsum(
         "acij,acjk->acik", mixing, columns.astype(jnp.float32), precision=lax.Precision.HIGHEST
     )
-    gathered = lax.all_gather(gathered, "arc", axis=0, tiled=True)
+    gathered = jnp.concatenate(
+        lax.all_to_all(jnp.stack([gathered] * lax.axis_size("arc")), "arc", 0, 0), axis=0
+    )
     row_data = from_root(gathered, "par", holder)
     row_flat = row_data.reshape(-1, row_block)
     col_flat = gathered.reshape(-1, col_block)

time: 482 us -> 618 us (1.28)
  waiting for transfers between devices: 377 us -> 501 us
  starting transfers between devices: 11.8 us -> 19.3 us
    all_to_all x0 -> x1, waiting for transfers between devices: none -> 201 us  [on_device(): lax.all_to_all(jnp.stack([gathered] * lax.axis_size('arc')), 'arc', 0, 0)]
    all_gather x1 -> x0, waiting for transfers between devices: 73.7 us -> none  [on_device(): gathered = lax.all_gather(gathered, 'arc', axis=0, tiled=True)]
    all_to_all x0 -> x1, starting transfers between devices: none -> 7.51 us  [on_device(): lax.all_to_all(jnp.stack([gathered] * lax.axis_size('arc')), 'arc', 0, 0)]
    unnamed x7 -> x9, local copies, waits for them, and re-layouts: 33.8 us -> 33.8 us
where the time goes in v1:
time: 618 us; the launch traced here: 616 us
  waiting for transfers between devices  501 us (81%)
  local copies, waits for them, and re-layouts  50.3 us (8%)
  matrix products  25.2 us (4%)
  starting transfers between devices  19.3 us (3%)
  between operations  13.5 us (2%)
  other arithmetic  7.55 us (1%)
    psum x1, waiting for transfers between devices, from_root(): return lax.psum(block, axis)  288 us
    all_to_all x1, waiting for transfers between devices, on_device(): lax.all_to_all(jnp.stack([gathered] * lax.axis_size('arc')), 'arc', 0, 0)  201 us
    unnamed x9, local copies, waits for them, and re-layouts  33.8 us
    dot_general x1, matrix products, on_device(): lax.dot_general(row_flat, col_flat, (((0,), (0,)), ((), ())), precision=l...  24.4 us
  transfers between devices with their start and end apart: 3, of which 3 were waited for; matrix products, arithmetic and copies ran while one was open for 0% of the time, Pallas kernels for 0%

profile of v1, /device:TPU:1, one launch (start us, length us, event | category | flops | bytes accessed | tf_op | source)
XLA Modules:
  0.0 616.4 jit_solution(1197837378569287326)
XLA Ops:
  6.5 0.0 copy-start
  6.5 0.0 copy-start.2
  6.5 9.5 %copy.4 = bf16[1,3,8,8192]{2,1,0,3:T(4,128)(2,1)} copy(bf16[1,3,8,8192]{3,2,1,0:T(8,128)(2,1)} %param.3) | data formatting | bytes 786432 | tf_op args[0]
  16.1 13.6 %reshape.232 = bf16[16,2,6144]{2,1,0:T(2,128)(2,1)} reshape(bf16[8192,1,3,8]{3,2,1,0:T(4,128)(2,1)} %bitcast.26) | data formatting | bytes 786432
  29.7 11.7 %all-to-all-start = ((bf16[16,2,6144]{2,1,0:T(2,128)(2,1)}), bf16[16,2,6144]{2,1,0:T(2,128)(2,1)S(1)}, u32[]{:S(2)}, u32[]{:S(2)}) async-start(bf16[16,2,6144]{2,1,0:T(2,128)(2,1)} %reshape.232), calls=%async_computation | async-start | bytes 786432 | tf_op jit(solution)/shard_map/all_to_all | solution.py:38
  41.4 0.0 copy-done.2
  41.4 0.2 fusion.4
  41.7 0.0 copy-done
  41.7 0.3 fusion
  42.0 11.7 %all-to-all-done = bf16[16,2,6144]{2,1,0:T(2,128)(2,1)S(1)} async-done(((bf16[16,2,6144]{2,1,0:T(2,128)(2,1)}), bf16[16,2,6144]{2,1,0:T(2,128)(2,1)S(1)}, u32[]{:S(2)}, u32[]{:S(2)}) %all-to-all-start) | async-done | bytes 393248 | tf_op jit(solution)/shard_map/all_to_all | solution.py:38
  53.7 10.7 %reshape.233 = bf16[8192,1,3,8]{3,2,1,0:T(4,128)(2,1)} reshape(bf16[16,2,6144]{2,1,0:T(2,128)(2,1)S(1)} %all-to-all-done) | data formatting | bytes 786432
  64.3 10.4 %copy.5 = bf16[1,3,8,16,512]{4,2,3,1,0:T(8,128)(2,1)S(1)} copy(bf16[1,3,8,16,512]{2,1,4,3,0:T(4,128)(2,1)} %bitcast.25) | data formatting | bytes 786432 | tf_op jit(solution)/shard_map/all_to_all | solution.py:38
  74.8 0.5 fusion.1
  75.3 6.1 stack.2
  81.3 7.5 %all-to-all-start.1 = ((f32[16,1,3,128,512]{4,3,2,1,0:T(8,128)}), f32[16,1,3,128,512]{4,3,2,1,0:T(8,128)}, u32[]{:S(2)}, u32[]{:S(2)}) async-start(f32[16,1,3,128,512]{4,3,2,1,0:T(8,128)} %stack.2), calls=%async_computation.1 | async-start | bytes 25165824 | tf_op jit(solution)/shard_map/all_to_all | solution.py:45
  88.9 0.0 all-reduce.2.cloned.1.call-start
  88.9 200.6 %all-to-all-done.1 = f32[16,1,3,128,512]{4,3,2,1,0:T(8,128)} async-done(((f32[16,1,3,128,512]{4,3,2,1,0:T(8,128)}), f32[16,1,3,128,512]{4,3,2,1,0:T(8,128)}, u32[]{:S(2)}, u32[]{:S(2)}) %all-to-all-start.1) | async-done | bytes 12582944 | tf_op jit(solution)/shard_map/all_to_all | solution.py:45
  289.5 7.3 %broadcast_select_fusion = f32[16,1,3,128,512]{4,3,2,1,0:T(8,128)} fusion(f32[16,1,3,128,512]{4,3,2,1,0:T(8,128)} %all-to-all-done.1, pred[]{:T(512)S(6)} %eq.21), kind=kLoop, calls=%fused_computation | loop fusion | flops 3145728 | bytes 25165824 | tf_op jit(solution)/shard_map/jit(_where)/select_n | solution.py:11
  296.9 0.0 all-reduce.2.cloned.1.call-update
  296.9 288.3 %all-reduce.2.cloned.1.call-done = f32[6144,512]{1,0:T(8,128)} async-done(((f32[6144,512]{1,0:T(8,128)}), f32[6144,512]{1,0:T(8,128)}) %all-reduce.2.cloned.1.call-update) | async-done | bytes 12582928 | tf_op jit(solution)/shard_map/psum | solution.py:12
  585.2 0.0 copy-start.1
  585.2 24.4 %fusion.5 = f32[512,512]{1,0:T(8,128)} fusion(f32[6144,512]{1,0:T(8,128)} %all-reduce.2.cloned.1.call-done, f32[6144,512]{1,0:T(8,128)} %bitcast.9), kind=kOutput, calls=%fused_computation.9 | convolution fusion | flops 19327352832 | bytes 26214400 | tf_op jit(solution)/shard_map/dot_general | solution.py:50
  609.6 0.0 copy-done.1
  (1 shorter events, 0.0 us)
Async XLA Ops:
  6.5 35.1 %copy-start = (f32[1,3,128,128]{3,2,1,0:T(8,128)S(1)}, f32[1,3,128,128]{3,2,1,0:T(8,128)}, u32[]{:S(2)}) copy-start(f32[1,3,128,128]{3,2,1,0:T(8,128)} %param.5) | copy-start | bytes 589828
  6.5 34.9 %copy-start.2 = (s32[1,128]{1,0:T(1,128)S(1)}, s32[1,128]{1,0:T(1,128)}, u32[]{:S(2)}) copy-start(s32[1,128]{1,0:T(1,128)} %param.4) | copy-start | bytes 1540
  29.7 24.0 %all-to-all-start = ((bf16[16,2,6144]{2,1,0:T(2,128)(2,1)}), bf16[16,2,6144]{2,1,0:T(2,128)(2,1)S(1)}, u32[]{:S(2)}, u32[]{:S(2)}) async-start(bf16[16,2,6144]{2,1,0:T(2,128)(2,1)} %reshape.232), calls=%async_computation | async-start | bytes 786432 | tf_op jit(solution)/shard_map/all_to_all | solution.py:38
  81.3 208.2 %all-to-all-start.1 = ((f32[16,1,3,128,512]{4,3,2,1,0:T(8,128)}), f32[16,1,3,128,512]{4,3,2,1,0:T(8,128)}, u32[]{:S(2)}, u32[]{:S(2)}) async-start(f32[16,1,3,128,512]{4,3,2,1,0:T(8,128)} %stack.2), calls=%async_computation.1 | async-start | bytes 25165824 | tf_op jit(solution)/shard_map/all_to_all | solution.py:45
  88.9 496.3 %all-reduce.2.cloned.1.call-start = ((), (), s32[]{:S(2)}) async-start(), calls=%async_computation.2 | async-start | bytes 25165824 | tf_op jit(solution)/shard_map/psum | solution.py:12
  585.2 24.4 %copy-start.1 = (f32[1,3,128,128]{3,2,1,0:T(8,128)S(1)}, f32[1,3,128,128]{3,2,1,0:T(8,128)}, u32[]{:S(2)}) copy-start(f32[1,3,128,128]{3,2,1,0:T(8,128)} %param.5) | copy-start | bytes 589828
Sparse Core Ops, SparseCore 0:
  297.0 288.1 all-reduce.1
